TPU v7x, 512 devices: a whole 4x4x16 slice. The times are simulated.
512 devices in a mesh: dp: 64 (over y, x, z_hi), tensor: 8 (over z_lo, core).
Axes of the slice: x: 4, y: 4, z: 16 (z_hi: 4, z_lo: 4; z = z_hi * 4 + z_lo), core: 2. Of those that a mesh axis runs over, the one named last changes fastest.
Arguments:
- inputs: bfloat16 [384, 16384], P('tensor', 'dp'), may hold values from -6 to 6
- out_grad: bfloat16 [384, 16384], P('tensor', 'dp'), may hold values from -6 to 6
- gate_weight: bfloat16 [16384, 8192], P('dp', 'tensor'), may hold values from -0.046875 to 0.046875
- up_weight: bfloat16 [16384, 8192], P('dp', 'tensor'), may hold values from -0.046875 to 0.046875
- down_weight: bfloat16 [8192, 16384], P('tensor', 'dp'), may hold values from -0.0625 to 0.0625
- segment_ids: int32 [384], P('tensor'), may hold values from 0 to 7, never falling along the last dimension, each value on 1 to 96 neighbouring positions
- token_weights: int32 [384], P('tensor'), may hold values from 1 to 16
Outputs:
- grad_gate: bfloat16 [16384, 8192], P('dp', 'tensor')
- grad_up: bfloat16 [16384, 8192], P('dp', 'tensor')
- grad_down: bfloat16 [8192, 16384], P('tensor', 'dp')
- grad_input: bfloat16 [384, 16384], P('tensor', 'dp')
Inputs may be any that keep to these rules, and one draw needn't show every extreme that they name: `segment_ids`: ids never fall along the tokens; each document holds 1 to 96 tokens.
All inputs are finite; a program needn't handle non-finite values.
Results may differ from a plain program's by a relative error of at most 0.0057.
Values may be sent and summed in bfloat16 or wider, within the bound.
No kernel may reach another device: no remote copies, remote signals or barrier semaphores. Data moves between devices by JAX's collectives and lax.ppermute only.
A program may use at most 64 MiB of HBM per device.

v0:
```python
import jax
import jax.numpy as jnp
from jax import lax
from jax.sharding import PartitionSpec as P


def token_scale(segment_ids, token_weights):
    same = segment_ids[:, None] == segment_ids[None, :]
    seg_total = jnp.sum(jnp.where(same, token_weights[None, :], 0), axis=1)
    seg_count = jnp.sum(same.astype(jnp.int32), axis=1)
    return (token_weights * seg_count).astype(jnp.float32) / seg_total.astype(jnp.float32)


def contract_last(left, right):
    return lax.dot_general(
        left, right, (((1,), (1,)), ((), ())), preferred_element_type=jnp.float32
    )


def contract_first(left, right):
    return lax.dot_general(
        left, right, (((0,), (0,)), ((), ())), preferred_element_type=jnp.float32
    )


def derivatives(hidden_grad, gate, up):
    sigma = jax.nn.sigmoid(gate)
    gate_grad = (hidden_grad * up * sigma * (1.0 + gate * (1.0 - sigma))).astype(jnp.bfloat16)
    up_grad = (hidden_grad * gate * sigma).astype(jnp.bfloat16)
    return (gate_grad, up_grad)


def shards(inputs, out_grad, gate_weight, up_weight, down_weight, segment_ids, token_weights):
    all_inputs, all_grads, all_ids, all_weights = (
        lax.all_gather(inputs, "tensor", axis=0, tiled=True),
        lax.all_gather(out_grad, "tensor", axis=0, tiled=True),
        lax.all_gather(segment_ids, "tensor", axis=0, tiled=True),
        lax.all_gather(token_weights, "tensor", axis=0, tiled=True),
    )
    scale = token_scale(all_ids, all_weights)
    weighted = (all_grads.astype(jnp.float32) * scale[:, None]).astype(jnp.bfloat16)
    gate_part = jnp.dot(all_inputs, gate_weight, preferred_element_type=jnp.float32)
    up_part = jnp.dot(all_inputs, up_weight, preferred_element_type=jnp.float32)
    gate, up = lax.psum((gate_part, up_part), "dp")
    hidden = (gate * jax.nn.sigmoid(gate) * up).astype(jnp.bfloat16)
    own_hidden = lax.psum_scatter(
        contract_last(weighted, down_weight), "dp", scatter_dimension=0, tiled=True
    )
    hidden_grad = lax.all_gather(own_hidden, "dp", axis=0, tiled=True)
    gate_grad, up_grad = derivatives(hidden_grad, gate, up)
    grad_down = contract_first(hidden, weighted).astype(jnp.bfloat16)
    grad_gate = contract_first(all_inputs, gate_grad).astype(jnp.bfloat16)
    grad_up = contract_first(all_inputs, up_grad).astype(jnp.bfloat16)
    grad_input = lax.psum_scatter(
        contract_last(gate_grad, gate_weight) + contract_last(up_grad, up_weight),
        "tensor",
        scatter_dimension=0,
        tiled=True,
    )
    return (grad_gate, grad_up, grad_down, grad_input.astype(jnp.bfloat16))


def solution(mesh):
    in_specs = (
        P("tensor", "dp"),
        P("tensor", "dp"),
        P("dp", "tensor"),
        P("dp", "tensor"),
        P("tensor", "dp"),
        P("tensor"),
        P("tensor"),
    )
    out_specs = (P("dp", "tensor"), P("dp", "tensor"), P("tensor", "dp"), P("tensor", "dp"))
    return jax.shard_map(shards, mesh=mesh, in_specs=in_specs, out_specs=out_specs, check_vma=False)
```

profile of v0, /device:TPU:1, one launch (start us, length us, event | category | flops | bytes accessed | tf_op | source)
XLA Modules:
  0.0 1386.3 jit_solution(15878878070452405531)
XLA Ops:
  7.2 21.2 %all_gather.15 = bf16[384,256]{1,0:T(8,128)(2,1)S(1)} all-gather(bf16[48,256]{1,0:T(8,128)(2,1)} %param.8), channel_id=1, replica_groups=mesh['dp'=64,'tensor'=8] {'tensor'}, dimensions={0}, use_global_device_ids=true | all-gather | bytes 221184 | tf_op jit(solution)/shard_map/all_gather | solution.py:36
  32.1 4.4 all-reduce.4
  36.8 1.5 fusion.5
  38.3 224.1 %fusion = f32[8,1024]{1,0:T(8,128)S(1)} fusion(f32[384,1024]{1,0:T(8,128)S(1)} %fusion.5), kind=kCustom, calls=%all-reduce-scatter | all-reduce-scatter fusion | flops 524289 | bytes 1607680
  266.3 1.4 collective-permute-start.12
  270.3 22.8 %collective-permute-start.9 = (f32[8,1024]{1,0:T(8,128)S(1)}, f32[8,1024]{1,0:T(8,128)S(1)}, u32[]{:S(2)}, u32[]{:S(2)}) collective-permute-start(f32[8,1024]{1,0:T(8,128)S(1)} %fusion), channel_id=1, source_target_pairs={{0,80},{8,88},{16,96},{24,104},{32,112},{40,120},{48,128},{56,136}... | collective-permute-start | bytes 98312
  295.7 3.7 collective-permute-start.6
  299.5 7.3 collective-permute-start.5
  306.8 3.3 collective-permute-start.4
  310.1 2.9 collective-permute-start.3
  313.0 2.7 collective-permute-start.2
  315.8 6.2 collective-permute-start.1
  322.0 7.0 collective-permute-start
  331.0 1.7 concatenate
  333.4 43.5 %all_gather.19 = bf16[384,256]{1,0:T(8,128)(2,1)S(1)} all-gather(bf16[48,256]{1,0:T(8,128)(2,1)S(1)} %copy-done.8), channel_id=1, replica_groups=mesh['dp'=64,'tensor'=8] {'tensor'}, dimensions={0}, use_global_device_ids=true | all-gather | bytes 221184 | tf_op jit(solution)/shard_map/all_gather | solution.py:35
  377.0 1.5 fusion.8
  378.5 1.6 fusion.7
  380.2 90.6 %all-gather.3.cloned.1.call-done = f32[64,6,1024]{2,1,0:T(8,128)} async-done(((f32[1,6,1024]{2,1,0:T(8,128)}), f32[64,6,1024]{2,1,0:T(8,128)}) %all-gather.3.cloned.1.call-update) | async-done | bytes 1572880 | tf_op jit(solution)/shard_map/all_gather | solution.py:49
  470.8 1.6 reshape.19
  472.4 824.1 %all-reduce.8.cloned.1.call-done = (f32[384,1024]{1,0:T(8,128)}, f32[384,1024]{1,0:T(8,128)}) async-done(((f32[384,1024]{1,0:T(8,128)}, f32[384,1024]{1,0:T(8,128)}), (f32[384,1024]{1,0:T(8,128)}, f32[384,1024]{1,0:T(8,128)})) %all-reduce.8.cloned.1.call-update) | async-done | bytes 3145744 | tf_op jit(solution)/shard_map/psum | solution.py:44
  1296.6 2.8 multiply_convert_fusion.1
  1304.8 3.4 convolution_convert_fusion
  1308.2 70.2 %reduce-scatter.4.cloned.1.call-done = f32[48,256]{1,0:T(8,128)} async-done(((f32[384,256]{1,0:T(8,128)}), f32[48,256]{1,0:T(8,128)}) %reduce-scatter.4.cloned.1.call-update) | async-done | bytes 49168 | tf_op jit(solution)/shard_map/reduce_scatter | solution.py:54
  1378.4 1.4 convert_element_type.55
  (63 shorter events, 19.9 us)
Async XLA Ops:
  7.2 369.8 %copy-start = (bf16[256,1024]{1,0:T(8,128)(2,1)S(1)}, bf16[256,1024]{1,0:T(8,128)(2,1)}, u32[]{:S(2)}) copy-start(bf16[256,1024]{1,0:T(8,128)(2,1)} %param.9) | copy-start | bytes 1572868
  7.2 463.6 %all-gather.3.cloned.1.call-start = ((), (), s32[]{:S(2)}) async-start(), calls=%async_computation.2 | async-start | bytes 2129920 | tf_op jit(solution)/shard_map/all_gather | solution.py:49
  28.4 233.9 %copy-start.6 = (bf16[384,256]{1,0:T(8,128)(2,1)}, bf16[384,256]{1,0:T(8,128)(2,1)S(1)}, u32[]{:S(2)}) copy-start(bf16[384,256]{1,0:T(8,128)(2,1)S(1)} %all_gather.15) | copy-start | bytes 589828
  38.2 295.2 %copy-start.8 = (bf16[48,256]{1,0:T(8,128)(2,1)S(1)}, bf16[48,256]{1,0:T(8,128)(2,1)}, u32[]{:S(2)}) copy-start(bf16[48,256]{1,0:T(8,128)(2,1)} %param.7) | copy-start | bytes 73732
  262.4 6.6 collective-permute-start.15
  263.7 6.6 collective-permute-start.14
  265.0 28.1 %collective-permute-start.13 = (f32[8,1024]{1,0:T(8,128)S(1)}, f32[8,1024]{1,0:T(8,128)S(1)}, u32[]{:S(2)}, u32[]{:S(2)}) collective-permute-start(f32[8,1024]{1,0:T(8,128)S(1)} %fusion), channel_id=1, source_target_pairs={{0,112},{8,120},{16,128},{24,136},{32,144},{40,152},{48,160},{56,1... | collective-permute-start | bytes 98312
  266.3 28.1 %collective-permute-start.12 = (f32[8,1024]{1,0:T(8,128)S(1)}, f32[8,1024]{1,0:T(8,128)S(1)}, u32[]{:S(2)}, u32[]{:S(2)}) collective-permute-start(f32[8,1024]{1,0:T(8,128)S(1)} %fusion), channel_id=1, source_target_pairs={{0,104},{8,112},{16,120},{24,128},{32,136},{40,144},{48,152},{56,1... | collective-permute-start | bytes 98312
  267.7 28.0 %collective-permute-start.11 = (f32[8,1024]{1,0:T(8,128)S(1)}, f32[8,1024]{1,0:T(8,128)S(1)}, u32[]{:S(2)}, u32[]{:S(2)}) collective-permute-start(f32[8,1024]{1,0:T(8,128)S(1)} %fusion), channel_id=1, source_target_pairs={{0,96},{8,104},{16,112},{24,120},{32,128},{40,136},{48,144},{56,15... | collective-permute-start | bytes 98312
  269.0 30.5 %collective-permute-start.10 = (f32[8,1024]{1,0:T(8,128)S(1)}, f32[8,1024]{1,0:T(8,128)S(1)}, u32[]{:S(2)}, u32[]{:S(2)}) collective-permute-start(f32[8,1024]{1,0:T(8,128)S(1)} %fusion), channel_id=1, source_target_pairs={{0,88},{8,96},{16,104},{24,112},{32,120},{40,128},{48,136},{56,144... | collective-permute-start | bytes 98312
  270.3 36.5 %collective-permute-start.9 = (f32[8,1024]{1,0:T(8,128)S(1)}, f32[8,1024]{1,0:T(8,128)S(1)}, u32[]{:S(2)}, u32[]{:S(2)}) collective-permute-start(f32[8,1024]{1,0:T(8,128)S(1)} %fusion), channel_id=1, source_target_pairs={{0,80},{8,88},{16,96},{24,104},{32,112},{40,120},{48,128},{56,136}... | collective-permute-start | bytes 98312
  293.1 17.0 %collective-permute-start.8 = (f32[8,1024]{1,0:T(8,128)S(1)}, f32[8,1024]{1,0:T(8,128)S(1)}, u32[]{:S(2)}, u32[]{:S(2)}) collective-permute-start(f32[8,1024]{1,0:T(8,128)S(1)} %fusion), channel_id=1, source_target_pairs={{0,72},{8,80},{16,88},{24,96},{32,104},{40,112},{48,120},{56,128},... | collective-permute-start | bytes 98312
  294.4 18.6 %collective-permute-start.7 = (f32[8,1024]{1,0:T(8,128)S(1)}, f32[8,1024]{1,0:T(8,128)S(1)}, u32[]{:S(2)}, u32[]{:S(2)}) collective-permute-start(f32[8,1024]{1,0:T(8,128)S(1)} %fusion), channel_id=1, source_target_pairs={{0,64},{8,72},{16,80},{24,88},{32,96},{40,104},{48,112},{56,120},{... | collective-permute-start | bytes 98312
  295.7 20.1 %collective-permute-start.6 = (f32[8,1024]{1,0:T(8,128)S(1)}, f32[8,1024]{1,0:T(8,128)S(1)}, u32[]{:S(2)}, u32[]{:S(2)}) collective-permute-start(f32[8,1024]{1,0:T(8,128)S(1)} %fusion), channel_id=1, source_target_pairs={{0,56},{8,64},{16,72},{24,80},{32,88},{40,96},{48,104},{56,112},{6... | collective-permute-start | bytes 98312
  299.5 22.5 %collective-permute-start.5 = (f32[8,1024]{1,0:T(8,128)S(1)}, f32[8,1024]{1,0:T(8,128)S(1)}, u32[]{:S(2)}, u32[]{:S(2)}) collective-permute-start(f32[8,1024]{1,0:T(8,128)S(1)} %fusion), channel_id=1, source_target_pairs={{0,48},{8,56},{16,64},{24,72},{32,80},{40,88},{48,96},{56,104},{64... | collective-permute-start | bytes 98312
  306.8 24.1 %collective-permute-start.4 = (f32[8,1024]{1,0:T(8,128)S(1)}, f32[8,1024]{1,0:T(8,128)S(1)}, u32[]{:S(2)}, u32[]{:S(2)}) collective-permute-start(f32[8,1024]{1,0:T(8,128)S(1)} %fusion), channel_id=1, source_target_pairs={{0,40},{8,48},{16,56},{24,64},{32,72},{40,80},{48,88},{56,96},{64,... | collective-permute-start | bytes 98312
  310.1 20.8 %collective-permute-start.3 = (f32[8,1024]{1,0:T(8,128)S(1)}, f32[8,1024]{1,0:T(8,128)S(1)}, u32[]{:S(2)}, u32[]{:S(2)}) collective-permute-start(f32[8,1024]{1,0:T(8,128)S(1)} %fusion), channel_id=1, source_target_pairs={{0,32},{8,40},{16,48},{24,56},{32,64},{40,72},{48,80},{56,88},{64,... | collective-permute-start | bytes 98312
  313.0 17.9 %collective-permute-start.2 = (f32[8,1024]{1,0:T(8,128)S(1)}, f32[8,1024]{1,0:T(8,128)S(1)}, u32[]{:S(2)}, u32[]{:S(2)}) collective-permute-start(f32[8,1024]{1,0:T(8,128)S(1)} %fusion), channel_id=1, source_target_pairs={{0,24},{8,32},{16,40},{24,48},{32,56},{40,64},{48,72},{56,80},{64,... | collective-permute-start | bytes 98312
  315.8 15.2 %collective-permute-start.1 = (f32[8,1024]{1,0:T(8,128)S(1)}, f32[8,1024]{1,0:T(8,128)S(1)}, u32[]{:S(2)}, u32[]{:S(2)}) collective-permute-start(f32[8,1024]{1,0:T(8,128)S(1)} %fusion), channel_id=1, source_target_pairs={{0,16},{8,24},{16,32},{24,40},{32,48},{40,56},{48,64},{56,72},{64,... | collective-permute-start | bytes 98312
  322.0 9.0 collective-permute-start
  332.7 45.8 %copy-start.3 = (bf16[256,1024]{1,0:T(8,128)(2,1)S(1)}, bf16[256,1024]{1,0:T(8,128)(2,1)}, u32[]{:S(2)}) copy-start(bf16[256,1024]{1,0:T(8,128)(2,1)} %param.10) | copy-start | bytes 1572868
  333.4 963.2 %all-reduce.8.cloned.1.call-start = ((), (), s32[]{:S(2)}) async-start(), calls=%async_computation.3 | async-start | bytes 6291456 | tf_op jit(solution)/shard_map/psum | solution.py:44
  377.0 1.5 copy-start.4
  380.1 998.2 %reduce-scatter.4.cloned.1.call-start = ((), (), s32[]{:S(2)}) async-start(), calls=%async_computation.1 | async-start | bytes 442368 | tf_op jit(solution)/shard_map/reduce_scatter | solution.py:54
  (4 other events, 4.8 us)
Sparse Core Ops, SparseCore 0:
  333.5 137.2 all-gather.2
  473.7 822.7 all-reduce.7
  1302.0 76.3 reduce-scatter.3
where the time goes:
time: 1390 us
  waiting for transfers between devices  985 us (71%)
  blocking collectives  293 us (21%)
  starting transfers between devices  66.5 us (5%)
  between operations  15.5 us (1%)
    psum x1, waiting for transfers between devices, shards(): gate, up = lax.psum((gate_part, up_part), 'dp')  824 us
    unnamed x2, blocking collectives  229 us
    all_gather x1, waiting for transfers between devices, shards(): hidden_grad = lax.all_gather(own_hidden, 'dp', axis=0, tiled=True)  90.6 us
    reduce_scatter x1, waiting for transfers between devices, shards(): lax.psum_scatter(contract_last(gate_grad, gate_weight) + contract_last(up...  70.2 us
    unnamed x16, starting transfers between devices  66.4 us
    all_gather x1, blocking collectives, shards(): lax.all_gather(inputs, 'tensor', axis=0, tiled=True)  43.5 us
  transfers between devices with their start and end apart: 19, of which 3 were waited for; matrix products, arithmetic and copies ran while one was open for 1% of the time, Pallas kernels for 0%

commit v1 on v0

v1 whole, which is shorter than its diff:
```python
import jax
import jax.numpy as jnp
from jax import lax
from jax.sharding import Mesh, PartitionSpec as P

YX = ("y", "x")
TENSOR = ("zl", "c")
TOKENS = 384
FF = 1024


def contract(left, right, dims):
    return lax.dot_general(left, right, (dims, ((), ())), preferred_element_type=jnp.float32)


def token_scale(ids, weights):
    same = ids[:, None] == ids[None, :]
    total = jnp.sum(jnp.where(same, weights[None, :], 0.0), axis=1)
    count = jnp.sum(same.astype(jnp.float32), axis=1)
    return weights * count / total


def derivatives(sums):
    gate, up, hidden_grad = jnp.split(sums, 3, axis=-1)
    sigma = jax.nn.sigmoid(gate)
    hidden = gate * sigma * up
    gate_grad = hidden_grad * up * sigma * (1.0 + gate * (1.0 - sigma))
    up_grad = hidden_grad * gate * sigma
    return jnp.concatenate([hidden, gate_grad, up_grad], axis=-1).astype(jnp.bfloat16)


def shards(inputs, out_grad, gate_weight, up_weight, down_weight, segment_ids, token_weights):
    side = jnp.stack([segment_ids, token_weights], axis=1).astype(jnp.bfloat16)
    side = jnp.pad(side, ((0, 0), (0, 126)))
    own = jnp.concatenate([inputs, out_grad, side], axis=1)
    every = lax.all_gather(own, TENSOR, axis=0, tiled=True)
    all_inputs, all_grads = every[:, :256], every[:, 256:512]
    scale = token_scale(every[:, 512].astype(jnp.float32), every[:, 513].astype(jnp.float32))
    weighted = (all_grads.astype(jnp.float32) * scale[:, None]).astype(jnp.bfloat16)

    parts = jnp.concatenate(
        [
            contract(all_inputs, gate_weight, ((1,), (0,))).astype(jnp.bfloat16),
            contract(all_inputs, up_weight, ((1,), (0,))).astype(jnp.bfloat16),
            contract(weighted, down_weight, ((1,), (1,))).astype(jnp.bfloat16),
        ],
        axis=1,
    )
    pieces = lax.all_to_all(parts.reshape(16, TOKENS // 16, 3 * FF), YX, 0, 0)
    partial = jnp.sum(pieces.astype(jnp.float32), axis=0).astype(jnp.bfloat16)
    partials = lax.all_gather(partial, "zh", axis=0)
    own_block = derivatives(jnp.sum(partials.astype(jnp.float32), axis=0))
    blocks = lax.all_to_all(jnp.broadcast_to(own_block[None], (16,) + own_block.shape), YX, 0, 0)
    blocks = blocks.reshape(TOKENS, 3 * FF)
    hidden, gate_grad, up_grad = blocks[:, :FF], blocks[:, FF : 2 * FF], blocks[:, 2 * FF :]

    back = contract(gate_grad, gate_weight, ((1,), (1,))) + contract(up_grad, up_weight, ((1,), (1,)))
    back = lax.all_to_all(back.reshape(8, TOKENS // 8, 256), TENSOR, 0, 0)
    grad_input = jnp.sum(back, axis=0).astype(jnp.bfloat16)
    grad_gate = contract(all_inputs, gate_grad, ((0,), (0,))).astype(jnp.bfloat16)
    grad_up = contract(all_inputs, up_grad, ((0,), (0,))).astype(jnp.bfloat16)
    grad_down = contract(hidden, weighted, ((0,), (0,))).astype(jnp.bfloat16)
    return grad_gate, grad_up, grad_down, grad_input


def solution(mesh):
    fine = Mesh(mesh.devices.reshape(4, 4, 4, 4, 2), ("y", "x", "zh", "zl", "c"))
    dp = ("y", "x", "zh")
    in_specs = (
        P(TENSOR, dp),
        P(TENSOR, dp),
        P(dp, TENSOR),
        P(dp, TENSOR),
        P(TENSOR, dp),
        P(TENSOR),
        P(TENSOR),
    )
    out_specs = (P(dp, TENSOR), P(dp, TENSOR), P(TENSOR, dp), P(TENSOR, dp))
    return jax.shard_map(shards, mesh=fine, in_specs=in_specs, out_specs=out_specs, check_vma=False)
```

time: 1390 us -> 150 us (0.11)
  waiting for transfers between devices: 985 us -> 7.96 us
  blocking collectives: 293 us -> 119 us
  starting transfers between devices: 66.5 us -> 8.91 us
  between operations: 15.5 us -> 0.77 us
    psum x1 -> x0, waiting for transfers between devices: 824 us -> none  [shards(): gate, up = lax.psum((gate_part, up_part), 'dp')]
    unnamed x2 -> x0, blocking collectives: 229 us -> none
    all_gather x1 -> x0, waiting for transfers between devices: 90.6 us -> none  [shards(): hidden_grad = lax.all_gather(own_hidden, 'dp', axis=0, tiled=True)]
    reduce_scatter x1 -> x0, waiting for transfers between devices: 70.2 us -> none  [shards(): lax.psum_scatter(contract_last(gate_grad, gate_weight) + contract_last(up...]
    unnamed x16 -> x0, starting transfers between devices: 66.4 us -> none
    all_to_all x0 -> x2, blocking collectives: none -> 65.5 us  [the longest x1 33.6 us: shards(): pieces = lax.all_to_all(parts.reshape(16, TOKENS // 16, 3 * FF), YX, 0, 0)]
  transfers between devices with their start and end apart: 19 -> 1, of which waited for: 3 -> 1; matrix products, arithmetic and copies ran while one was open for 1% -> 3% of each run, Pallas kernels for 0% -> 0%
where the time goes in v1:
time: 150 us; the launch traced here: 149 us
  blocking collectives  119 us (79%)
  starting transfers between devices  8.91 us (6%)
  waiting for transfers between devices  7.96 us (5%)
  matrix products  7.59 us (5%)
  other arithmetic  4.35 us (3%)
    all_to_all x1, blocking collectives, shards(): pieces = lax.all_to_all(parts.reshape(16, TOKENS // 16, 3 * FF), YX, 0, 0)  33.6 us
    all_gather x1, blocking collectives, shards(): partials = lax.all_gather(partial, 'zh', axis=0)  32.2 us
    all_to_all x1, blocking collectives, shards(): lax.all_to_all(jnp.broadcast_to(own_block[None], (16,) + own_block.shape)...  31.9 us
    all_gather x1, blocking collectives, shards(): every = lax.all_gather(own, TENSOR, axis=0, tiled=True)  21.6 us
    all_to_all x1, starting transfers between devices, shards(): back = lax.all_to_all(back.reshape(8, TOKENS // 8, 256), TENSOR, 0, 0)  8.91 us
    all_to_all x1, waiting for transfers between devices, shards(): back = lax.all_to_all(back.reshape(8, TOKENS // 8, 256), TENSOR, 0, 0)  7.96 us
    dot_general x8, matrix products, contract(): lax.dot_general(left, right, (dims, ((), ())), preferred_element_type=jnp...  7.59 us
  transfers between devices with their start and end apart: 1, of which 1 were waited for; matrix products, arithmetic and copies ran while one was open for 3% of the time, Pallas kernels for 0%

profile of v1, /device:TPU:1, one launch (start us, length us, event | category | flops | bytes accessed | tf_op | source)
XLA Modules:
  0.0 149.4 jit_solution(4474488378374229905)
XLA Ops:
  0.7 0.8 convert_bitcast_fusion
  1.4 0.1 copy.19
  1.5 0.8 fusion.13
  2.3 21.6 %all_gather.9 = bf16[384,640]{1,0:T(8,128)(2,1)S(1)} all-gather(bf16[48,640]{1,0:T(8,128)(2,1)S(1)} %fusion.13), channel_id=1, replica_groups=mesh['y'=4,'x'=4,'zh'=4,'zl'=4,'c'=2] {'zl','c'}, dimensions={0}, use_global_device_ids=true | all-gather | bytes 552960 | tf_op jit(solution)/shard_map/all_gather | solution.py:36
  23.9 0.1 convert_reduce_fusion.1
  24.0 0.1 slice.30
  24.3 1.4 convolution_convert_fusion.1
  25.7 0.4 convolution_convert_fusion.2
  26.1 0.3 fusion.6
  26.4 0.4 convolution_convert_fusion
  26.8 0.2 pad_maximum_fusion
  27.0 33.6 %all_to_all.15 = bf16[16,24,3072]{2,1,0:T(8,128)(2,1)S(1)} all-to-all(bf16[16,24,3072]{2,1,0:T(8,128)(2,1)S(1)} %bitcast.14), channel_id=1, replica_groups=mesh['y'=4,'x'=4,'zh'=4,'zl'=4,'c'=2] {'y','x'}, dimensions={0} | all-to-all | bytes 4718592 | tf_op jit(solution)/shard_map/all_to_all | solution.py:49
  60.6 0.4 reduce_sum.56
  61.0 32.2 %all-gather = bf16[96,3072]{1,0:T(8,128)(2,1)S(1)} all-gather(bf16[24,3072]{1,0:T(8,128)(2,1)S(1)} %reduce_sum.56), channel_id=2, replica_groups=mesh['y'=4,'x'=4,'zh'=4,'zl'=4,'c'=2] {'zh'}, dimensions={0}, use_global_device_ids=true | all-gather | bytes 737280 | tf_op jit(solution)/shard_map/all_gather | solution.py:51
  93.4 0.3 broadcast_in_dim.24
  93.7 31.9 %all_to_all.16 = bf16[16,24,3072]{2,1,0:T(8,128)(2,1)S(1)} all-to-all(bf16[16,24,3072]{2,1,0:T(8,128)(2,1)S(1)} %broadcast_in_dim.24), channel_id=1, replica_groups=mesh['y'=4,'x'=4,'zh'=4,'zl'=4,'c'=2] {'y','x'}, dimensions={0} | all-to-all | bytes 4718592 | tf_op jit(solution)/shard_map/all_to_all | solution.py:53
  125.5 0.4 fusion.3
  126.0 1.2 convolution_add_fusion
  127.1 8.9 %all-to-all-start.2 = ((f32[8,48,256]{2,1,0:T(8,128)}), f32[8,48,256]{2,1,0:T(8,128)}, u32[]{:S(2)}, u32[]{:S(2)}) async-start(f32[8,48,256]{2,1,0:T(8,128)} %bitcast.21), calls=%async_computation.2 | async-start | bytes 786432 | tf_op jit(solution)/shard_map/all_to_all | solution.py:58
  136.0 1.3 convolution_convert_fusion.4
  137.3 1.3 convolution_convert_fusion.5
  138.5 1.3 convolution_convert_fusion.3
  139.9 8.0 %all-to-all-done.2 = f32[8,48,256]{2,1,0:T(8,128)} async-done(((f32[8,48,256]{2,1,0:T(8,128)}), f32[8,48,256]{2,1,0:T(8,128)}, u32[]{:S(2)}, u32[]{:S(2)}) %all-to-all-start.2) | async-done | bytes 393248 | tf_op jit(solution)/shard_map/all_to_all | solution.py:58
  147.8 1.6 %reduce_sum.58 = bf16[48,256]{1,0:T(8,128)(2,1)} reduce(f32[8,48,256]{2,1,0:T(8,128)} %all-to-all-done.2, f32[]{:T(128)} %constant.6.clone.1), dimensions={0}, to_apply=%region_4.5 | reduce | flops 86016 | bytes 417796 | tf_op jit(solution)/shard_map/reduce_sum | solution.py:59
  (13 shorter events, 0.4 us)
Async XLA Ops:
  0.6 25.1 %copy-start = (bf16[256,1024]{1,0:T(8,128)(2,1)S(1)}, bf16[256,1024]{1,0:T(8,128)(2,1)}, u32[]{:S(2)}) copy-start(bf16[256,1024]{1,0:T(8,128)(2,1)} %param.9) | copy-start | bytes 1572868
  0.6 25.8 %copy-start.2 = (bf16[1024,256]{1,0:T(8,128)(2,1)S(1)}, bf16[1024,256]{1,0:T(8,128)(2,1)}, u32[]{:S(2)}) copy-start(bf16[1024,256]{1,0:T(8,128)(2,1)} %param.11) | copy-start | bytes 1572868
  93.7 32.3 %copy-start.1 = (bf16[256,1024]{1,0:T(8,128)(2,1)S(1)}, bf16[256,1024]{1,0:T(8,128)(2,1)}, u32[]{:S(2)}) copy-start(bf16[256,1024]{1,0:T(8,128)(2,1)} %param.10) | copy-start | bytes 1572868
  127.1 20.7 %all-to-all-start.2 = ((f32[8,48,256]{2,1,0:T(8,128)}), f32[8,48,256]{2,1,0:T(8,128)}, u32[]{:S(2)}, u32[]{:S(2)}) async-start(f32[8,48,256]{2,1,0:T(8,128)} %bitcast.21), calls=%async_computation.2 | async-start | bytes 786432 | tf_op jit(solution)/shard_map/all_to_all | solution.py:58

commit v2 on v1

--- a/solution.py
+++ b/solution.py
@@ -55,8 +55,8 @@
     hidden, gate_grad, up_grad = blocks[:, :FF], blocks[:, FF : 2 * FF], blocks[:, 2 * FF :]
 
     back = contract(gate_grad, gate_weight, ((1,), (1,))) + contract(up_grad, up_weight, ((1,), (1,)))
-    back = lax.all_to_all(back.reshape(8, TOKENS // 8, 256), TENSOR, 0, 0)
-    grad_input = jnp.sum(back, axis=0).astype(jnp.bfloat16)
+    back = lax.all_to_all(back.astype(jnp.bfloat16).reshape(8, TOKENS // 8, 256), TENSOR, 0, 0)
+    grad_input = jnp.sum(back.astype(jnp.float32), axis=0).astype(jnp.bfloat16)
     grad_gate = contract(all_inputs, gate_grad, ((0,), (0,))).astype(jnp.bfloat16)
     grad_up = contract(all_inputs, up_grad, ((0,), (0,))).astype(jnp.bfloat16)
     grad_down = contract(hidden, weighted, ((0,), (0,))).astype(jnp.bfloat16)

time: 150 us -> 145 us (0.967)
  waiting for transfers between devices: 7.96 us -> 2.73 us
    all_to_all x1, waiting for transfers between devices: 7.96 us -> 2.73 us  [shards(): lax.all_to_all(back.astype(jnp.bfloat16).reshape(8, TOKENS // 8, 256), TE...]
where the time goes in v2:
time: 145 us; the launch traced here: 144 us
  blocking collectives  119 us (82%)
  starting transfers between devices  8.89 us (6%)
  matrix products  7.59 us (5%)
  other arithmetic  4.26 us (3%)
  waiting for transfers between devices  2.73 us (2%)
    all_to_all x1, blocking collectives, shards(): pieces = lax.all_to_all(parts.reshape(16, TOKENS // 16, 3 * FF), YX, 0, 0)  33.6 us
    all_to_all x1, blocking collectives, shards(): lax.all_to_all(jnp.broadcast_to(own_block[None], (16,) + own_block.shape)...  32.3 us
    all_gather x1, blocking collectives, shards(): partials = lax.all_gather(partial, 'zh', axis=0)  31.8 us
    all_gather x1, blocking collectives, shards(): every = lax.all_gather(own, TENSOR, axis=0, tiled=True)  21.6 us
    all_to_all x1, starting transfers between devices, shards(): lax.all_to_all(back.astype(jnp.bfloat16).reshape(8, TOKENS // 8, 256), TE...  8.89 us
    dot_general x8, matrix products, contract(): lax.dot_general(left, right, (dims, ((), ())), preferred_element_type=jnp...  7.59 us
  transfers between devices with their start and end apart: 1, of which 1 were waited for; matrix products, arithmetic and copies ran while one was open for 3% of the time, Pallas kernels for 0%

profile of v2, /device:TPU:1, one launch (start us, length us, event | category | flops | bytes accessed | tf_op | source)
XLA Modules:
  0.0 144.2 jit_solution(8073862819107298397)
XLA Ops:
  0.6 0.7 convert_bitcast_fusion
  1.4 0.1 copy.19
  1.5 0.8 fusion.14
  2.3 21.6 %all_gather.9 = bf16[384,640]{1,0:T(8,128)(2,1)S(1)} all-gather(bf16[48,640]{1,0:T(8,128)(2,1)S(1)} %fusion.14), channel_id=1, replica_groups=mesh['y'=4,'x'=4,'zh'=4,'zl'=4,'c'=2] {'zl','c'}, dimensions={0}, use_global_device_ids=true | all-gather | bytes 552960 | tf_op jit(solution)/shard_map/all_gather | solution.py:36
  23.9 0.1 convert_reduce_fusion.1
  24.0 0.1 slice.30
  24.2 1.5 %convolution_convert_fusion.1 = bf16[384,1024]{1,0:T(8,128)(2,1)S(1)} fusion(bf16[256,1024]{1,0:T(8,128)(2,1)} %param.10, bf16[384,640]{1,0:T(8,128)(2,1)S(1)} %all_gather.9), kind=kOutput, calls=%fused_computation.2 | convolution fusion | flops 201719808 | bytes 1507328 | tf_op jit(solution)/shard_map/dot_general | solution.py:13
  25.7 0.4 convolution_convert_fusion.2
  26.1 0.3 fusion.7
  26.4 0.4 convolution_convert_fusion
  26.8 0.2 pad_maximum_fusion
  27.0 33.6 %all_to_all.15 = bf16[16,24,3072]{2,1,0:T(8,128)(2,1)S(1)} all-to-all(bf16[16,24,3072]{2,1,0:T(8,128)(2,1)S(1)} %bitcast.14), channel_id=1, replica_groups=mesh['y'=4,'x'=4,'zh'=4,'zl'=4,'c'=2] {'y','x'}, dimensions={0} | all-to-all | bytes 4718592 | tf_op jit(solution)/shard_map/all_to_all | solution.py:49
  60.6 0.4 reduce_sum.59
  61.0 31.8 %all-gather = bf16[96,3072]{1,0:T(8,128)(2,1)S(1)} all-gather(bf16[24,3072]{1,0:T(8,128)(2,1)S(1)} %reduce_sum.59), channel_id=2, replica_groups=mesh['y'=4,'x'=4,'zh'=4,'zl'=4,'c'=2] {'zh'}, dimensions={0}, use_global_device_ids=true | all-gather | bytes 737280 | tf_op jit(solution)/shard_map/all_gather | solution.py:51
  93.0 0.3 broadcast_in_dim.24
  93.3 32.3 %all_to_all.16 = bf16[16,24,3072]{2,1,0:T(8,128)(2,1)S(1)} all-to-all(bf16[16,24,3072]{2,1,0:T(8,128)(2,1)S(1)} %broadcast_in_dim.24), channel_id=1, replica_groups=mesh['y'=4,'x'=4,'zh'=4,'zl'=4,'c'=2] {'y','x'}, dimensions={0} | all-to-all | bytes 4718592 | tf_op jit(solution)/shard_map/all_to_all | solution.py:53
  125.6 0.4 fusion.4
  126.0 1.1 fusion
  127.1 8.9 %all-to-all-start.2 = ((bf16[8,48,256]{2,1,0:T(8,128)(2,1)}), bf16[8,48,256]{2,1,0:T(8,128)(2,1)}, u32[]{:S(2)}, u32[]{:S(2)}) async-start(bf16[8,48,256]{2,1,0:T(8,128)(2,1)} %bitcast.21), calls=%async_computation.2 | async-start | bytes 393216 | tf_op jit(solution)/shard_map/all_to_all | solution.py:58
  136.0 1.3 convolution_convert_fusion.4
  137.3 1.3 convolution_convert_fusion.5
  138.5 1.3 convolution_convert_fusion.3
  139.9 2.7 %all-to-all-done.2 = bf16[8,48,256]{2,1,0:T(8,128)(2,1)} async-done(((bf16[8,48,256]{2,1,0:T(8,128)(2,1)}), bf16[8,48,256]{2,1,0:T(8,128)(2,1)}, u32[]{:S(2)}, u32[]{:S(2)}) %all-to-all-start.2) | async-done | bytes 196640 | tf_op jit(solution)/shard_map/all_to_all | solution.py:58
  142.6 1.6 %reduce_sum.61 = bf16[48,256]{1,0:T(8,128)(2,1)} reduce(bf16[8,48,256]{2,1,0:T(8,128)(2,1)} %all-to-all-done.2, bf16[]{:T(256)} %constant.6.clone.1), dimensions={0}, to_apply=%region_4.5 | reduce | flops 86016 | bytes 221186 | tf_op jit(solution)/shard_map/reduce_sum | solution.py:59
  (13 shorter events, 0.3 us)
Async XLA Ops:
  0.6 25.1 %copy-start = (bf16[256,1024]{1,0:T(8,128)(2,1)S(1)}, bf16[256,1024]{1,0:T(8,128)(2,1)}, u32[]{:S(2)}) copy-start(bf16[256,1024]{1,0:T(8,128)(2,1)} %param.9) | copy-start | bytes 1572868
  24.2 2.2 %copy-start.2 = (bf16[1024,256]{1,0:T(8,128)(2,1)S(1)}, bf16[1024,256]{1,0:T(8,128)(2,1)}, u32[]{:S(2)}) copy-start(bf16[1024,256]{1,0:T(8,128)(2,1)} %param.11) | copy-start | bytes 1572868
  93.3 32.7 %copy-start.1 = (bf16[256,1024]{1,0:T(8,128)(2,1)S(1)}, bf16[256,1024]{1,0:T(8,128)(2,1)}, u32[]{:S(2)}) copy-start(bf16[256,1024]{1,0:T(8,128)(2,1)} %param.10) | copy-start | bytes 1572868
  127.1 15.5 %all-to-all-start.2 = ((bf16[8,48,256]{2,1,0:T(8,128)(2,1)}), bf16[8,48,256]{2,1,0:T(8,128)(2,1)}, u32[]{:S(2)}, u32[]{:S(2)}) async-start(bf16[8,48,256]{2,1,0:T(8,128)(2,1)} %bitcast.21), calls=%async_computation.2 | async-start | bytes 393216 | tf_op jit(solution)/shard_map/all_to_all | solution.py:58

commit v3 on v2

--- a/solution.py
+++ b/solution.py
@@ -3,8 +3,8 @@
 from jax import lax
 from jax.sharding import Mesh, PartitionSpec as P
 
-YX = ("y", "x")
-TENSOR = ("zl", "c")
+YX = ("x", "y")
+TENSOR = ("zm", "zl", "c")
 TOKENS = 384
 FF = 1024
 
@@ -46,6 +46,7 @@
         ],
         axis=1,
     )
+    parts, weighted, all_inputs = lax.optimization_barrier((parts, weighted, all_inputs))
     pieces = lax.all_to_all(parts.reshape(16, TOKENS // 16, 3 * FF), YX, 0, 0)
     partial = jnp.sum(pieces.astype(jnp.float32), axis=0).astype(jnp.bfloat16)
     partials = lax.all_gather(partial, "zh", axis=0)
@@ -55,7 +56,8 @@
     hidden, gate_grad, up_grad = blocks[:, :FF], blocks[:, FF : 2 * FF], blocks[:, 2 * FF :]
 
     back = contract(gate_grad, gate_weight, ((1,), (1,))) + contract(up_grad, up_weight, ((1,), (1,)))
-    back = lax.all_to_all(back.astype(jnp.bfloat16).reshape(8, TOKENS // 8, 256), TENSOR, 0, 0)
+    back = back.astype(jnp.bfloat16).reshape(2, 2, 2, TOKENS // 8, 256).swapaxes(0, 1).reshape(8, TOKENS // 8, 256)
+    back = lax.all_to_all(back, ("zl", "zm", "c"), 0, 0)
     grad_input = jnp.sum(back.astype(jnp.float32), axis=0).astype(jnp.bfloat16)
     grad_gate = contract(all_inputs, gate_grad, ((0,), (0,))).astype(jnp.bfloat16)
     grad_up = contract(all_inputs, up_grad, ((0,), (0,))).astype(jnp.bfloat16)
@@ -64,7 +66,7 @@
 
 
 def solution(mesh):
-    fine = Mesh(mesh.devices.reshape(4, 4, 4, 4, 2), ("y", "x", "zh", "zl", "c"))
+    fine = Mesh(mesh.devices.reshape(4, 4, 4, 2, 2, 2), ("y", "x", "zh", "zm", "zl", "c"))
     dp = ("y", "x", "zh")
     in_specs = (
         P(TENSOR, dp),

time: 145 us -> 141 us (0.972)
  matrix products: 7.59 us -> 5.73 us
    dot_general x8, matrix products: 7.59 us -> 5.73 us  [contract(): lax.dot_general(left, right, (dims, ((), ())), preferred_element_type=jnp...]
where the time goes in v3:
time: 141 us
  blocking collectives  118 us (84%)
  starting transfers between devices  9.25 us (7%)
  matrix products  5.73 us (4%)
  other arithmetic  3.48 us (2%)
  waiting for transfers between devices  2.2 us (2%)
    all_to_all x1, blocking collectives, shards(): pieces = lax.all_to_all(parts.reshape(16, TOKENS // 16, 3 * FF), YX, 0, 0)  33 us
    all_gather x1, blocking collectives, shards(): partials = lax.all_gather(partial, 'zh', axis=0)  31.7 us
    all_to_all x1, blocking collectives, shards(): lax.all_to_all(jnp.broadcast_to(own_block[None], (16,) + own_block.shape)...  31.3 us
    all_gather x1, blocking collectives, shards(): every = lax.all_gather(own, TENSOR, axis=0, tiled=True)  21.8 us
    all_to_all x1, starting transfers between devices, shards(): back = lax.all_to_all(back, ('zl', 'zm', 'c'), 0, 0)  9.25 us
    dot_general x8, matrix products, contract(): lax.dot_general(left, right, (dims, ((), ())), preferred_element_type=jnp...  5.73 us
  transfers between devices with their start and end apart: 1, of which 1 were waited for; matrix products, arithmetic and copies ran while one was open for 3% of the time, Pallas kernels for 0%

profile of v3, /device:TPU:1, one launch (start us, length us, event | category | flops | bytes accessed | tf_op | source)
XLA Modules:
  0.0 140.6 jit_solution(16190066218261062142)
XLA Ops:
  0.7 0.8 convert_bitcast_fusion
  1.5 0.8 fusion.10
  2.3 21.8 %all_gather.9 = bf16[384,640]{1,0:T(8,128)(2,1)S(1)} all-gather(bf16[48,640]{1,0:T(8,128)(2,1)S(1)} %fusion.10), channel_id=1, replica_groups=mesh['y'=4,'x'=4,'zh'=4,'zm'=2,'zl'=2,'c'=2] {'zm','zl','c'}, dimensions={0}, use_global_device_ids=true | all-gather | bytes 552960 | tf_op jit(solution)/shard_map/all_gather | solution.py:36
  24.1 0.1 convert_reduce_fusion.1
  24.4 0.3 fusion.7
  24.8 0.1 multiply_convert_fusion
  24.9 0.4 convolution_convert_fusion.2
  25.3 0.4 convolution_convert_fusion.1
  25.7 0.4 convolution_convert_fusion
  26.1 0.2 pad_maximum_fusion
  26.3 33.0 %all_to_all.15 = bf16[16,24,3072]{2,1,0:T(8,128)(2,1)S(1)} all-to-all(bf16[16,24,3072]{2,1,0:T(8,128)(2,1)S(1)} %bitcast.21), channel_id=1, replica_groups=mesh['y'=4,'x'=4,'zh'=4,'zm'=2,'zl'=2,'c'=2] {'x','y'}, dimensions={0} | all-to-all | bytes 4718592 | tf_op jit(solution)/shard_map/all_to_all | solution.py:50
  59.3 0.4 reduce_sum.59
  59.7 31.7 %all-gather = bf16[96,3072]{1,0:T(8,128)(2,1)S(1)} all-gather(bf16[24,3072]{1,0:T(8,128)(2,1)S(1)} %reduce_sum.59), channel_id=2, replica_groups=mesh['y'=4,'x'=4,'zh'=4,'zm'=2,'zl'=2,'c'=2] {'zh'}, dimensions={0}, use_global_device_ids=true | all-gather | bytes 737280 | tf_op jit(solution)/shard_map/all_gather | solution.py:52
  91.5 0.3 broadcast_in_dim.24
  91.8 31.3 %all_to_all.16 = bf16[16,24,3072]{2,1,0:T(8,128)(2,1)S(1)} all-to-all(bf16[16,24,3072]{2,1,0:T(8,128)(2,1)S(1)} %broadcast_in_dim.24), channel_id=1, replica_groups=mesh['y'=4,'x'=4,'zh'=4,'zm'=2,'zl'=2,'c'=2] {'x','y'}, dimensions={0} | all-to-all | bytes 4718592 | tf_op jit(solution)/shard_map/all_to_all | solution.py:54
  123.2 0.4 fusion.4
  123.6 0.4 fusion
  124.0 0.7 copy.20
  124.7 9.2 %all-to-all-start.2 = ((bf16[8,48,256]{2,1,0:T(8,128)(2,1)}), bf16[8,48,256]{2,1,0:T(8,128)(2,1)S(1)}, u32[]{:S(2)}, u32[]{:S(2)}) async-start(bf16[8,48,256]{2,1,0:T(8,128)(2,1)} %bitcast.7), calls=%async_computation.2 | async-start | bytes 393216 | tf_op jit(solution)/shard_map/all_to_all | solution.py:60
  134.0 1.3 convolution_convert_fusion.4
  135.2 1.3 convolution_convert_fusion.5
  136.5 1.3 convolution_convert_fusion.3
  137.7 2.2 %all-to-all-done.2 = bf16[8,48,256]{2,1,0:T(8,128)(2,1)S(1)} async-done(((bf16[8,48,256]{2,1,0:T(8,128)(2,1)}), bf16[8,48,256]{2,1,0:T(8,128)(2,1)S(1)}, u32[]{:S(2)}, u32[]{:S(2)}) %all-to-all-start.2) | async-done | bytes 196640 | tf_op jit(solution)/shard_map/all_to_all | solution.py:60
  139.9 0.6 reduce_sum.61
  (18 shorter events, 0.6 us)
Async XLA Ops:
  0.6 24.3 %copy-start = (bf16[256,1024]{1,0:T(8,128)(2,1)S(1)}, bf16[256,1024]{1,0:T(8,128)(2,1)}, u32[]{:S(2)}) copy-start(bf16[256,1024]{1,0:T(8,128)(2,1)} %param.9) | copy-start | bytes 1572868
  0.6 24.6 %copy-start.2 = (bf16[256,1024]{1,0:T(8,128)(2,1)S(1)}, bf16[256,1024]{1,0:T(8,128)(2,1)}, u32[]{:S(2)}) copy-start(bf16[256,1024]{1,0:T(8,128)(2,1)} %param.10) | copy-start | bytes 1572868
  2.3 23.4 %copy-start.1 = (bf16[1024,256]{1,0:T(8,128)(2,1)S(1)}, bf16[1024,256]{1,0:T(8,128)(2,1)}, u32[]{:S(2)}) copy-start(bf16[1024,256]{1,0:T(8,128)(2,1)} %param.11) | copy-start | bytes 1572868
  91.8 31.8 %copy-start.3 = (bf16[256,1024]{1,0:T(8,128)(2,1)S(1)}, bf16[256,1024]{1,0:T(8,128)(2,1)}, u32[]{:S(2)}) copy-start(bf16[256,1024]{1,0:T(8,128)(2,1)} %param.10) | copy-start | bytes 1572868
  124.7 15.2 %all-to-all-start.2 = ((bf16[8,48,256]{2,1,0:T(8,128)(2,1)}), bf16[8,48,256]{2,1,0:T(8,128)(2,1)S(1)}, u32[]{:S(2)}, u32[]{:S(2)}) async-start(bf16[8,48,256]{2,1,0:T(8,128)(2,1)} %bitcast.7), calls=%async_computation.2 | async-start | bytes 393216 | tf_op jit(solution)/shard_map/all_to_all | solution.py:60

commit v4 on v3

--- a/solution.py
+++ b/solution.py
@@ -30,12 +30,15 @@
 
 
 def shards(inputs, out_grad, gate_weight, up_weight, down_weight, segment_ids, token_weights):
-    side = jnp.stack([segment_ids, token_weights], axis=1).astype(jnp.bfloat16)
-    side = jnp.pad(side, ((0, 0), (0, 126)))
+    token = lax.broadcasted_iota(jnp.int32, (TOKENS // 8, 128), 0)
+    lane = lax.broadcasted_iota(jnp.int32, (TOKENS // 8, 128), 1)
+    codes = jnp.pad(segment_ids, (0, 80)) + jnp.pad(token_weights, (64, 16))
+    side = jnp.where((lane & 63) == token, codes[None, :], 0).astype(jnp.bfloat16)
     own = jnp.concatenate([inputs, out_grad, side], axis=1)
     every = lax.all_gather(own, TENSOR, axis=0, tiled=True)
     all_inputs, all_grads = every[:, :256], every[:, 256:512]
-    scale = token_scale(every[:, 512].astype(jnp.float32), every[:, 513].astype(jnp.float32))
+    sides = every[:, 512:].astype(jnp.float32)
+    scale = token_scale(jnp.sum(sides[:, :64], axis=1), jnp.sum(sides[:, 64:], axis=1))
     weighted = (all_grads.astype(jnp.float32) * scale[:, None]).astype(jnp.bfloat16)
 
     parts = jnp.concatenate(
@@ -48,9 +51,10 @@
     )
     parts, weighted, all_inputs = lax.optimization_barrier((parts, weighted, all_inputs))
     pieces = lax.all_to_all(parts.reshape(16, TOKENS // 16, 3 * FF), YX, 0, 0)
-    partial = jnp.sum(pieces.astype(jnp.float32), axis=0).astype(jnp.bfloat16)
-    partials = lax.all_gather(partial, "zh", axis=0)
-    own_block = derivatives(jnp.sum(partials.astype(jnp.float32), axis=0))
+    own_sum = jnp.sum(pieces.astype(jnp.float32), axis=0)
+    rounded = lax.reduce_precision(own_sum, 8, 7)
+    partials = lax.all_gather(rounded.astype(jnp.bfloat16), "zh", axis=0)
+    own_block = derivatives(jnp.sum(partials.astype(jnp.float32), axis=0) + (own_sum - rounded))
     blocks = lax.all_to_all(jnp.broadcast_to(own_block[None], (16,) + own_block.shape), YX, 0, 0)
     blocks = blocks.reshape(TOKENS, 3 * FF)
     hidden, gate_grad, up_grad = blocks[:, :FF], blocks[:, FF : 2 * FF], blocks[:, 2 * FF :]

time: 141 us -> 141 us (level)
  no operation moved by 1% of the time
where the time goes in v4:
time: 141 us; the launch traced here: 140 us
  blocking collectives  118 us (84%)
  starting transfers between devices  9.58 us (7%)
  matrix products  5.73 us (4%)
  other arithmetic  3.69 us (3%)
  waiting for transfers between devices  2.2 us (2%)
    all_to_all x1, blocking collectives, shards(): pieces = lax.all_to_all(parts.reshape(16, TOKENS // 16, 3 * FF), YX, 0, 0)  33 us
    all_gather x1, blocking collectives, shards(): partials = lax.all_gather(rounded.astype(jnp.bfloat16), 'zh', axis=0)  31.5 us
    all_to_all x1, blocking collectives, shards(): lax.all_to_all(jnp.broadcast_to(own_block[None], (16,) + own_block.shape)...  31.3 us
    all_gather x1, blocking collectives, shards(): every = lax.all_gather(own, TENSOR, axis=0, tiled=True)  21.6 us
    all_to_all x1, starting transfers between devices, shards(): back = lax.all_to_all(back, ('zl', 'zm', 'c'), 0, 0)  9.58 us
    dot_general x8, matrix products, contract(): lax.dot_general(left, right, (dims, ((), ())), preferred_element_type=jnp...  5.73 us
  transfers between devices with their start and end apart: 1, of which 1 were waited for; matrix products, arithmetic and copies ran while one was open for 3% of the time, Pallas kernels for 0%

profile of v4, /device:TPU:1, one launch (start us, length us, event | category | flops | bytes accessed | tf_op | source)
XLA Modules:
  0.0 140.5 jit_solution(9007957339960358278)
XLA Ops:
  0.7 0.8 pad_add_fusion
  1.5 0.8 pad_maximum_fusion.2
  2.3 21.6 %all_gather.7 = bf16[384,640]{1,0:T(8,128)(2,1)S(1)} all-gather(bf16[48,640]{1,0:T(8,128)(2,1)S(1)} %pad_maximum_fusion.2), channel_id=1, replica_groups=mesh['y'=4,'x'=4,'zh'=4,'zm'=2,'zl'=2,'c'=2] {'zm','zl','c'}, dimensions={0}, use_global_device_ids=true | all-gather | bytes 552960 | tf_op jit(solution)/shard_map/all_gather | solution.py:38
  23.9 0.3 slice_reduce_fusion
  24.2 0.3 fusion.7
  24.5 0.1 multiply_convert_fusion
  24.6 0.4 convolution_convert_fusion.2
  25.0 0.4 convolution_convert_fusion.1
  25.4 0.4 convolution_convert_fusion
  25.8 0.2 pad_maximum_fusion
  26.0 33.0 %all_to_all.15 = bf16[16,24,3072]{2,1,0:T(8,128)(2,1)S(1)} all-to-all(bf16[16,24,3072]{2,1,0:T(8,128)(2,1)S(1)} %bitcast.17), channel_id=1, replica_groups=mesh['y'=4,'x'=4,'zh'=4,'zm'=2,'zl'=2,'c'=2] {'x','y'}, dimensions={0} | all-to-all | bytes 4718592 | tf_op jit(solution)/shard_map/all_to_all | solution.py:53
  59.0 0.4 convert_reduce_fusion
  59.4 31.5 %all-gather = bf16[96,3072]{1,0:T(8,128)(2,1)S(1)} all-gather(bf16[24,3072]{1,0:T(8,128)(2,1)S(1)} %reduce-precision_convert_fusion), channel_id=2, replica_groups=mesh['y'=4,'x'=4,'zh'=4,'zm'=2,'zl'=2,'c'=2] {'zh'}, dimensions={0}, use_global_device_ids=true | all-gather | bytes 737280 | tf_op jit(solution)/shard_map/all_gather | solution.py:56
  91.2 0.3 broadcast_in_dim.39
  91.4 31.3 %all_to_all.16 = bf16[16,24,3072]{2,1,0:T(8,128)(2,1)S(1)} all-to-all(bf16[16,24,3072]{2,1,0:T(8,128)(2,1)S(1)} %broadcast_in_dim.39), channel_id=1, replica_groups=mesh['y'=4,'x'=4,'zh'=4,'zm'=2,'zl'=2,'c'=2] {'x','y'}, dimensions={0} | all-to-all | bytes 4718592 | tf_op jit(solution)/shard_map/all_to_all | solution.py:58
  122.8 0.4 fusion.4
  123.2 0.4 fusion
  123.6 0.7 copy.12
  124.3 9.6 %all-to-all-start.2 = ((bf16[8,48,256]{2,1,0:T(8,128)(2,1)}), bf16[8,48,256]{2,1,0:T(8,128)(2,1)S(1)}, u32[]{:S(2)}, u32[]{:S(2)}) async-start(bf16[8,48,256]{2,1,0:T(8,128)(2,1)} %bitcast.5), calls=%async_computation.2 | async-start | bytes 393216 | tf_op jit(solution)/shard_map/all_to_all | solution.py:64
  133.9 1.3 convolution_convert_fusion.4
  135.1 1.3 convolution_convert_fusion.5
  136.4 1.3 convolution_convert_fusion.3
  137.6 2.2 %all-to-all-done.2 = bf16[8,48,256]{2,1,0:T(8,128)(2,1)S(1)} async-done(((bf16[8,48,256]{2,1,0:T(8,128)(2,1)}), bf16[8,48,256]{2,1,0:T(8,128)(2,1)S(1)}, u32[]{:S(2)}, u32[]{:S(2)}) %all-to-all-start.2) | async-done | bytes 196640 | tf_op jit(solution)/shard_map/all_to_all | solution.py:64
  139.8 0.6 reduce_sum.72
  (15 shorter events, 0.3 us)
Async XLA Ops:
  0.6 24.0 %copy-start = (bf16[256,1024]{1,0:T(8,128)(2,1)S(1)}, bf16[256,1024]{1,0:T(8,128)(2,1)}, u32[]{:S(2)}) copy-start(bf16[256,1024]{1,0:T(8,128)(2,1)} %param.9) | copy-start | bytes 1572868
  0.6 24.4 %copy-start.2 = (bf16[256,1024]{1,0:T(8,128)(2,1)S(1)}, bf16[256,1024]{1,0:T(8,128)(2,1)}, u32[]{:S(2)}) copy-start(bf16[256,1024]{1,0:T(8,128)(2,1)} %param.10) | copy-start | bytes 1572868
  23.9 1.5 %copy-start.1 = (bf16[1024,256]{1,0:T(8,128)(2,1)S(1)}, bf16[1024,256]{1,0:T(8,128)(2,1)}, u32[]{:S(2)}) copy-start(bf16[1024,256]{1,0:T(8,128)(2,1)} %param.11) | copy-start | bytes 1572868
  124.3 15.5 %all-to-all-start.2 = ((bf16[8,48,256]{2,1,0:T(8,128)(2,1)}), bf16[8,48,256]{2,1,0:T(8,128)(2,1)S(1)}, u32[]{:S(2)}, u32[]{:S(2)}) async-start(bf16[8,48,256]{2,1,0:T(8,128)(2,1)} %bitcast.5), calls=%async_computation.2 | async-start | bytes 393216 | tf_op jit(solution)/shard_map/all_to_all | solution.py:64

commit v5 on v4

--- a/solution.py
+++ b/solution.py
@@ -1,6 +1,8 @@
 import jax
 import jax.numpy as jnp
 from jax import lax
+from jax.experimental import pallas as pl
+from jax.experimental.pallas import tpu as pltpu
 from jax.sharding import Mesh, PartitionSpec as P
 
 YX = ("x", "y")
@@ -20,13 +22,36 @@
     return weights * count / total
 
 
-def derivatives(sums):
-    gate, up, hidden_grad = jnp.split(sums, 3, axis=-1)
-    sigma = jax.nn.sigmoid(gate)
-    hidden = gate * sigma * up
-    gate_grad = hidden_grad * up * sigma * (1.0 + gate * (1.0 - sigma))
-    up_grad = hidden_grad * gate * sigma
-    return jnp.concatenate([hidden, gate_grad, up_grad], axis=-1).astype(jnp.bfloat16)
+def spread_kernel(partials, rest, out):
+    for at in range(0, FF, 256):
+        sums = []
+        for kind in range(3):
+            cut = slice(kind * FF + at, kind * FF + at + 256)
+            total = rest[:, cut]
+            for plane in range(4):
+                total = total + partials[plane, :, cut].astype(jnp.float32)
+            sums.append(total)
+        gate, up, hidden_grad = sums
+        sigma = jax.nn.sigmoid(gate)
+        up_grad = hidden_grad * gate * sigma
+        hidden = gate * sigma * up
+        gate_grad = hidden_grad * up * sigma * (1.0 + gate * (1.0 - sigma))
+        for kind, value in enumerate((hidden, gate_grad, up_grad)):
+            value = value.astype(jnp.bfloat16)
+            for copy in range(16):
+                out[copy, :, kind * FF + at : kind * FF + at + 256] = value
+
+
+def spread(partials, rest):
+    vmem = pl.BlockSpec(memory_space=pltpu.VMEM)
+    return pl.pallas_call(
+        spread_kernel,
+        out_shape=jax.ShapeDtypeStruct((16,) + rest.shape, jnp.bfloat16),
+        in_specs=[vmem, vmem],
+        out_specs=vmem,
+        compiler_params=pltpu.CompilerParams(vmem_limit_bytes=16 * 1024 * 1024),
+        name="spread",
+    )(partials, rest)
 
 
 def shards(inputs, out_grad, gate_weight, up_weight, down_weight, segment_ids, token_weights):
@@ -54,8 +79,7 @@
     own_sum = jnp.sum(pieces.astype(jnp.float32), axis=0)
     rounded = lax.reduce_precision(own_sum, 8, 7)
     partials = lax.all_gather(rounded.astype(jnp.bfloat16), "zh", axis=0)
-    own_block = derivatives(jnp.sum(partials.astype(jnp.float32), axis=0) + (own_sum - rounded))
-    blocks = lax.all_to_all(jnp.broadcast_to(own_block[None], (16,) + own_block.shape), YX, 0, 0)
+    blocks = lax.all_to_all(spread(partials, own_sum - rounded), YX, 0, 0)
     blocks = blocks.reshape(TOKENS, 3 * FF)
     hidden, gate_grad, up_grad = blocks[:, :FF], blocks[:, FF : 2 * FF], blocks[:, 2 * FF :]
 

time: 141 us -> 141 us (level)
  no operation moved by 1% of the time
where the time goes in v5:
time: 141 us; the launch traced here: 140 us
  blocking collectives  118 us (84%)
  starting transfers between devices  9.56 us (7%)
  matrix products  5.73 us (4%)
  other arithmetic  3.5 us (2%)
  waiting for transfers between devices  2.2 us (2%)
    all_to_all x1, blocking collectives, shards(): pieces = lax.all_to_all(parts.reshape(16, TOKENS // 16, 3 * FF), YX, 0, 0)  33 us
    all_gather x1, blocking collectives, shards(): partials = lax.all_gather(rounded.astype(jnp.bfloat16), 'zh', axis=0)  31.5 us
    all_to_all x1, blocking collectives, shards(): blocks = lax.all_to_all(spread(partials, own_sum - rounded), YX, 0, 0)  31.3 us
    all_gather x1, blocking collectives, shards(): every = lax.all_gather(own, TENSOR, axis=0, tiled=True)  21.6 us
    all_to_all x1, starting transfers between devices, shards(): back = lax.all_to_all(back, ('zl', 'zm', 'c'), 0, 0)  9.56 us
    dot_general x8, matrix products, contract(): lax.dot_general(left, right, (dims, ((), ())), preferred_element_type=jnp...  5.73 us
  transfers between devices with their start and end apart: 1, of which 1 were waited for; matrix products, arithmetic and copies ran while one was open for 3% of the time, Pallas kernels for 0%

profile of v5, /device:TPU:1, one launch (start us, length us, event | category | flops | bytes accessed | tf_op | source)
XLA Modules:
  0.0 140.3 jit_solution(9473037126816451022)
XLA Ops:
  0.7 0.8 pad_add_fusion
  1.5 0.8 pad_maximum_fusion.1
  2.3 21.6 %all_gather.7 = bf16[384,640]{1,0:T(8,128)(2,1)S(1)} all-gather(bf16[48,640]{1,0:T(8,128)(2,1)S(1)} %pad_maximum_fusion.1), channel_id=1, replica_groups=mesh['y'=4,'x'=4,'zh'=4,'zm'=2,'zl'=2,'c'=2] {'zm','zl','c'}, dimensions={0}, use_global_device_ids=true | all-gather | bytes 552960 | tf_op jit(solution)/shard_map/all_gather | solution.py:63
  23.9 0.3 slice_reduce_fusion
  24.2 0.3 fusion.7
  24.5 0.1 multiply_convert_fusion
  24.6 0.4 convolution_convert_fusion.2
  25.0 0.4 convolution_convert_fusion.1
  25.4 0.4 convolution_convert_fusion
  25.8 0.2 pad_maximum_fusion
  26.0 33.0 %all_to_all.15 = bf16[16,24,3072]{2,1,0:T(8,128)(2,1)S(1)} all-to-all(bf16[16,24,3072]{2,1,0:T(8,128)(2,1)S(1)} %bitcast.17), channel_id=1, replica_groups=mesh['y'=4,'x'=4,'zh'=4,'zm'=2,'zl'=2,'c'=2] {'x','y'}, dimensions={0} | all-to-all | bytes 4718592 | tf_op jit(solution)/shard_map/all_to_all | solution.py:78
  59.0 0.4 convert_reduce_fusion
  59.4 31.5 %all-gather = bf16[96,3072]{1,0:T(8,128)(2,1)S(1)} all-gather(bf16[24,3072]{1,0:T(8,128)(2,1)S(1)} %get-tuple-element.15), channel_id=2, replica_groups=mesh['y'=4,'x'=4,'zh'=4,'zm'=2,'zl'=2,'c'=2] {'zh'}, dimensions={0}, use_global_device_ids=true | all-gather | bytes 737280 | tf_op jit(solution)/shard_map/all_gather | solution.py:81
  91.0 0.3 spread.1
  91.3 31.3 %all_to_all.16 = bf16[16,24,3072]{2,1,0:T(8,128)(2,1)S(1)} all-to-all(bf16[16,24,3072]{2,1,0:T(8,128)(2,1)S(1)} %spread.1), channel_id=1, replica_groups=mesh['y'=4,'x'=4,'zh'=4,'zm'=2,'zl'=2,'c'=2] {'x','y'}, dimensions={0} | all-to-all | bytes 4718592 | tf_op jit(solution)/shard_map/all_to_all | solution.py:82
  122.6 0.4 fusion.4
  123.0 0.4 fusion
  123.5 0.7 copy.12
  124.1 9.6 %all-to-all-start.2 = ((bf16[8,48,256]{2,1,0:T(8,128)(2,1)}), bf16[8,48,256]{2,1,0:T(8,128)(2,1)S(1)}, u32[]{:S(2)}, u32[]{:S(2)}) async-start(bf16[8,48,256]{2,1,0:T(8,128)(2,1)} %bitcast.5), calls=%async_computation.2 | async-start | bytes 393216 | tf_op jit(solution)/shard_map/all_to_all | solution.py:88
  133.7 1.3 convolution_convert_fusion.4
  135.0 1.3 convolution_convert_fusion.5
  136.2 1.3 convolution_convert_fusion.3
  137.5 2.2 %all-to-all-done.2 = bf16[8,48,256]{2,1,0:T(8,128)(2,1)S(1)} async-done(((bf16[8,48,256]{2,1,0:T(8,128)(2,1)}), bf16[8,48,256]{2,1,0:T(8,128)(2,1)S(1)}, u32[]{:S(2)}, u32[]{:S(2)}) %all-to-all-start.2) | async-done | bytes 196640 | tf_op jit(solution)/shard_map/all_to_all | solution.py:88
  139.7 0.6 reduce_sum.62
  (11 shorter events, 0.1 us)
Async XLA Ops:
  0.6 24.0 %copy-start = (bf16[256,1024]{1,0:T(8,128)(2,1)S(1)}, bf16[256,1024]{1,0:T(8,128)(2,1)}, u32[]{:S(2)}) copy-start(bf16[256,1024]{1,0:T(8,128)(2,1)} %param.9) | copy-start | bytes 1572868
  0.6 24.4 %copy-start.2 = (bf16[256,1024]{1,0:T(8,128)(2,1)S(1)}, bf16[256,1024]{1,0:T(8,128)(2,1)}, u32[]{:S(2)}) copy-start(bf16[256,1024]{1,0:T(8,128)(2,1)} %param.10) | copy-start | bytes 1572868
  23.9 1.5 %copy-start.1 = (bf16[1024,256]{1,0:T(8,128)(2,1)S(1)}, bf16[1024,256]{1,0:T(8,128)(2,1)}, u32[]{:S(2)}) copy-start(bf16[1024,256]{1,0:T(8,128)(2,1)} %param.11) | copy-start | bytes 1572868
  124.1 15.5 %all-to-all-start.2 = ((bf16[8,48,256]{2,1,0:T(8,128)(2,1)}), bf16[8,48,256]{2,1,0:T(8,128)(2,1)S(1)}, u32[]{:S(2)}, u32[]{:S(2)}) async-start(bf16[8,48,256]{2,1,0:T(8,128)(2,1)} %bitcast.5), calls=%async_computation.2 | async-start | bytes 393216 | tf_op jit(solution)/shard_map/all_to_all | solution.py:88
